TPU v7x, 32 devices: a whole 2x2x4 slice. The times are simulated.
32 devices in a mesh: blk: 8 (over z, y), rank: 4 (over x, core).
Axes of the slice: x: 2, y: 2, z: 4, core: 2. Of those that a mesh axis runs over, the one named last changes fastest.
Arguments:
- user_factors: float32 [256, 4096], P('rank', 'blk'), may hold values from -1.5 to 1.5
- item_factors: float32 [256, 8192], P('rank', 'blk'), may hold values from -1.5 to 1.5
- tile_rows: int32 [8, 4, 4096], P('blk'), may hold values from 0 to 511
- tile_cols: int32 [8, 4, 4096], P('blk'), may hold values from 0 to 1023
- tile_vals: float32 [8, 4, 4096], P('blk'), may hold values from -4 to 4
- tile_count: int32 [8, 4], P('blk'), may hold values from 512 to 4096, as said below
Outputs:
- new_users: float32 [256, 4096], P('rank', 'blk')
- new_items: float32 [256, 8192], P('rank', 'blk')
Inputs may be any that keep to these rules, and one draw needn't show every extreme that they name: `tile_count`: in every stratum some block's tile is full (4096 live slots).
All inputs are finite; a program needn't handle non-finite values.
Results may differ from a plain program's by a relative error of at most 0.0003.
Values sent between devices are 32-bit elements; how exact they have to be, the bound alone decides.
A program may use at most 64 MiB of HBM per device.

v0:
```python
import functools

import jax
import jax.numpy as jnp
from jax import lax
from jax.experimental import pallas as pl
from jax.experimental.pallas import tpu as pltpu
from jax.sharding import PartitionSpec as P

BATCH = 1024
LANES = 128
GROUPS = BATCH // LANES
CHUNK = 256
HALVES = 1
HALF = BATCH // HALVES
HALF_GROUPS = GROUPS // HALVES
LEARN_RATE = 0.05
DECAY_WEIGHT = 0.02
MESH = pl.DeviceIdType.MESH


def split_rows(block):
    high = block.astype(jnp.bfloat16)
    low = (block - high.astype(jnp.float32)).astype(jnp.bfloat16)
    return high, low


def kernel(
    blocks, ranks,
    u_in, v_in, rows_in, cols_in, vals_in, count_in,
    u_out, v_out,
    rows, cols, vals, count, users, u_cat, v_cat, held, tiles, chooser, spreader, u_pick, v_pick, u_step, v_step,
    partial, arrived, errs,
    part_send, part_recv, tile_send, tile_recv, user_send, user_recv, load_sem,
):
    depth, user_count = u_in.shape
    item_count = v_in.shape[1]
    strata, tile = rows_in.shape[1:]
    per_tile = tile // BATCH
    spans = tile // LANES
    batches = strata * per_tile
    blk = lax.axis_index("blk")
    rank = lax.axis_index("rank")

    def at_blk(shift):
        return (lax.rem(blk + (shift % blocks), blocks), rank)

    def at_rank(shift):
        return (blk, lax.rem(rank + (shift % ranks), ranks))

    barrier = pltpu.get_barrier_semaphore()
    met = [at_rank(o) for o in range(1, ranks)]
    met += [at_blk(o) for o in range(1, strata)] + [at_blk(-o) for o in range(1, strata)]
    for device in met:
        pl.semaphore_signal(barrier, inc=1, device_id=device, device_id_type=MESH)

    loads = [
        pltpu.make_async_copy(source, target, load_sem.at[i])
        for i, (source, target) in enumerate(
            (
                (count_in, count), (rows_in, rows), (cols_in, cols), (vals_in, vals),
                (u_in, users.at[0]), (v_in, v_out),
            )
        )
    ]
    for load in loads:
        load.start()
    for load in loads[:4]:
        load.wait()

    stratum_at = lax.broadcasted_iota(jnp.int32, (strata, LANES), 0)
    lane_at = lax.broadcasted_iota(jnp.int32, (strata, LANES), 1)
    live = jnp.zeros((strata, LANES), jnp.int32)
    for s in range(strata):
        live = jnp.where(stratum_at == s, count[0, s], live)
    for r in range(spans):
        here = slice(r * LANES, (r + 1) * LANES)
        alive = lane_at + r * LANES < live
        held[:, r, :] = jnp.where(alive, rows[0, :, here], -1).astype(jnp.float32)
        held[:, spans + r, :] = jnp.where(alive, cols[0, :, here], -1).astype(jnp.float32)
        held[:, 2 * spans + r, :] = vals[0, :, here]
    tiles[0] = held[0]

    parts = ((0, user_count, 0), (user_count, item_count, spans))
    down = lax.broadcasted_iota(jnp.int32, (CHUNK, LANES), 0)
    across = lax.broadcasted_iota(jnp.int32, (LANES, LANES), 1)

    def chosen(place, index):
        return jnp.where(place == index, 1.0, 0.0).astype(jnp.bfloat16)

    def index_of(s, q, first):
        at = pl.multiple_of(first + q * GROUPS, GROUPS)
        return tiles[s, pl.ds(at, GROUPS), :].astype(jnp.int32)

    def build_chooser(s, q):
        for base, size, first in parts:
            index = index_of(s, q, first)
            for j in range(GROUPS):
                row = jnp.broadcast_to(index[j : j + 1, :], (CHUNK, LANES))
                for t in range(0, size, CHUNK):
                    chooser[base + t : base + t + CHUNK, j * LANES : (j + 1) * LANES] = (
                        chosen(down + t, row)
                    )

    def build_spreader(s, q):
        for base, size, first in parts:
            index = jnp.transpose(index_of(s, q, first))
            for j in range(GROUPS):
                column = jnp.broadcast_to(index[:, j : j + 1], (LANES, LANES))
                for t in range(0, size, LANES):
                    spreader[j * LANES : (j + 1) * LANES, base + t : base + t + LANES] = (
                        chosen(across + t, column)
                    )

    def cut_users(s):
        high, low = split_rows(users[s])
        u_cat[:depth] = high
        u_cat[depth:] = low

    build_chooser(0, 0)
    for load in loads[4:]:
        load.wait()
    cut_users(0)
    high, low = split_rows(v_out[...])
    v_cat[:depth] = high
    v_cat[depth:] = low

    def tile_copy(s):
        return pltpu.make_async_remote_copy(
            src_ref=held.at[s], dst_ref=tiles.at[s],
            send_sem=tile_send.at[s], recv_sem=tile_recv.at[s],
            device_id=(lax.rem(blk + blocks - s, blocks), rank),
            device_id_type=MESH,
        )

    def user_copy(s):
        return pltpu.make_async_remote_copy(
            src_ref=users.at[s], dst_ref=users.at[s + 1],
            send_sem=user_send.at[s], recv_sem=user_recv.at[s],
            device_id=at_blk(-1), device_id_type=MESH,
        )

    def home():
        return pltpu.make_async_remote_copy(
            src_ref=users.at[strata - 1], dst_ref=u_out,
            send_sem=user_send.at[strata - 1], recv_sem=user_recv.at[strata - 1],
            device_id=at_blk(strata - 1), device_id_type=MESH,
        )

    def part_copy(slot, h, o):
        return pltpu.make_async_remote_copy(
            src_ref=partial.at[slot, h], dst_ref=arrived.at[slot, h, o - 1],
            send_sem=part_send.at[slot, h, o - 1], recv_sem=part_recv.at[slot, h, o - 1],
            device_id=at_rank(o), device_id_type=MESH,
        )

    group_at = lax.broadcasted_iota(jnp.int32, (HALF_GROUPS, LANES), 0)

    @pl.loop(0, batches)
    def _(k):
        s = k // per_tile
        q = k % per_tile
        slot = k % 2
        totals = []
        for h in range(HALVES):
            total = jnp.zeros((HALF_GROUPS, LANES), jnp.float32)
            for c in range(h * HALF, (h + 1) * HALF, CHUNK):
                here = slice(c, c + CHUNK)
                u = jnp.dot(u_cat[...], chooser[:user_count, here], preferred_element_type=jnp.float32)
                u = u[:depth] + u[depth:]
                v = jnp.dot(v_cat[...], chooser[user_count:, here], preferred_element_type=jnp.float32)
                v = v[:depth] + v[depth:]
                u_pick[:, here] = u
                v_pick[:, here] = v
                sums = jnp.sum(u * v, axis=0, keepdims=True)
                for g in range(0, CHUNK, LANES):
                    total = jnp.where(
                        group_at == (c - h * HALF + g) // LANES, sums[:, g : g + LANES], total
                    )
            partial[slot, h] = total
            if h == 0:

                @pl.when(k == 0)
                def _():
                    pl.semaphore_wait(barrier, len(met))

            for o in range(1, ranks):
                part_copy(slot, h, o).start()
            totals.append(total)
        turn = jnp.logical_and(q == per_tile - 1, s < strata - 1)

        @pl.when(k == 0)
        def _():
            for other in range(1, strata):
                tile_copy(other).start()

        build_spreader(s, q)

        @pl.when(turn)
        def _():
            tile_copy(s + 1).wait_recv()

        @pl.when(k < batches - 1)
        def _():
            build_chooser((k + 1) // per_tile, (k + 1) % per_tile)

        for h in range(HALVES):
            total = totals[h]
            for o in range(1, ranks):
                part_copy(slot, h, o).wait_recv()
                total = total + arrived[slot, h, o - 1]
            at = pl.multiple_of(2 * spans + q * GROUPS, GROUPS)
            targets = tiles[s, pl.ds(at, GROUPS), :]
            errs[h] = LEARN_RATE * (targets[h * HALF_GROUPS : (h + 1) * HALF_GROUPS] - total)
            for j in range(HALF_GROUPS):
                here = slice(h * HALF + j * LANES, h * HALF + (j + 1) * LANES)
                e = errs[h, j : j + 1, :]
                u = u_pick[:, here]
                v = v_pick[:, here]
                high, low = split_rows(e * v - LEARN_RATE * DECAY_WEIGHT * u)
                u_step[:depth, here] = high
                u_step[depth:, here] = low
            span = slice(h * HALF, (h + 1) * HALF)
            last = h == HALVES - 1

            def spread(steps, first):
                moved = jnp.dot(
                    steps[:, span], spreader[span, first : first + CHUNK],
                    preferred_element_type=jnp.float32,
                )
                return moved[:depth] + moved[depth:]

            for t in range(0, user_count, CHUNK):
                here = slice(t, t + CHUNK)
                new = users[s, :, here] + spread(u_step, t)
                users[s, :, here] = new
                if last:
                    high, low = split_rows(new)
                    u_cat[:depth, here] = high
                    u_cat[depth:, here] = low
            if last:

                @pl.when(turn)
                def _():
                    user_copy(s).start()

                @pl.when(k == batches - 1)
                def _():
                    home().start()

            for j in range(HALF_GROUPS):
                here = slice(h * HALF + j * LANES, h * HALF + (j + 1) * LANES)
                e = errs[h, j : j + 1, :]
                u = u_pick[:, here]
                v = v_pick[:, here]
                high, low = split_rows(e * u - LEARN_RATE * DECAY_WEIGHT * v)
                v_step[:depth, here] = high
                v_step[depth:, here] = low

            for t in range(0, item_count, CHUNK):
                here = slice(t, t + CHUNK)
                new = v_out[:, here] + spread(v_step, user_count + t)
                v_out[:, here] = new
                if last:
                    high, low = split_rows(new)
                    v_cat[:depth, here] = high
                    v_cat[depth:, here] = low

        for h in range(HALVES):
            for o in range(1, ranks):
                part_copy(slot, h, o).wait_send()

        @pl.when(turn)
        def _():
            user_copy(s).wait()
            cut_users(s + 1)

    for s in range(1, strata):
        tile_copy(s).wait_send()
    home().wait()


def solution(mesh):
    blocks, ranks = mesh.shape["blk"], mesh.shape["rank"]

    def per_device(user_factors, item_factors, tile_rows, tile_cols, tile_vals, tile_count):
        depth, user_count = user_factors.shape
        item_count = item_factors.shape[1]
        strata, tile = tile_rows.shape[1:]
        held = (strata, 3 * tile // LANES, LANES)
        vmem = pl.BlockSpec(memory_space=pltpu.VMEM)
        f32, bf16 = jnp.float32, jnp.bfloat16
        return pl.pallas_call(
            functools.partial(kernel, blocks, ranks),
            out_shape=(
                jax.ShapeDtypeStruct((depth, user_count), f32),
                jax.ShapeDtypeStruct((depth, item_count), f32),
            ),
            in_specs=[pl.BlockSpec(memory_space=pl.ANY)] * 6,
            out_specs=(vmem, vmem),
            scratch_shapes=[
                pltpu.VMEM(tile_rows.shape, jnp.int32),
                pltpu.VMEM(tile_cols.shape, jnp.int32),
                pltpu.VMEM(tile_vals.shape, f32),
                pltpu.SMEM(tile_count.shape, jnp.int32),
                pltpu.VMEM((strata, depth, user_count), f32),
                pltpu.VMEM((2 * depth, user_count), bf16),
                pltpu.VMEM((2 * depth, item_count), bf16),
                pltpu.VMEM(held, f32),
                pltpu.VMEM(held, f32),
                pltpu.VMEM((user_count + item_count, BATCH), bf16),
                pltpu.VMEM((BATCH, user_count + item_count), bf16),
                pltpu.VMEM((depth, BATCH), f32),
                pltpu.VMEM((depth, BATCH), f32),
                pltpu.VMEM((2 * depth, BATCH), bf16),
                pltpu.VMEM((2 * depth, BATCH), bf16),
                pltpu.VMEM((2, HALVES, HALF_GROUPS, LANES), f32),
                pltpu.VMEM((2, HALVES, ranks - 1, HALF_GROUPS, LANES), f32),
                pltpu.VMEM((HALVES, HALF_GROUPS, LANES), f32),
                pltpu.SemaphoreType.DMA((2, HALVES, ranks - 1)),
                pltpu.SemaphoreType.DMA((2, HALVES, ranks - 1)),
                pltpu.SemaphoreType.DMA((strata,)),
                pltpu.SemaphoreType.DMA((strata,)),
                pltpu.SemaphoreType.DMA((strata,)),
                pltpu.SemaphoreType.DMA((strata,)),
                pltpu.SemaphoreType.DMA((6,)),
            ],
            compiler_params=pltpu.CompilerParams(
                collective_id=0, has_side_effects=True, vmem_limit_bytes=60 * 1024 * 1024
            ),
        )(user_factors, item_factors, tile_rows, tile_cols, tile_vals, tile_count)

    placed = (
        P("rank", "blk"),
        P("rank", "blk"),
        P("blk", None, None),
        P("blk", None, None),
        P("blk", None, None),
        P("blk", None),
    )
    return jax.shard_map(
        per_device,
        mesh=mesh,
        in_specs=placed,
        out_specs=(P("rank", "blk"), P("rank", "blk")),
        check_vma=False,
    )
```

profile of v0, /device:TPU:0, one launch (start us, length us, event | category | flops | bytes accessed | tf_op | source)
XLA Modules:
  0.0 96.5 jit_solution(17513110026318044980)
XLA Ops:
  0.6 93.5 %shard_map.77 = (f32[64,512]{1,0:T(8,128)}, f32[64,1024]{1,0:T(8,128)}) custom-call(f32[64,512]{1,0:T(8,128)} %u_in.1, f32[64,1024]{1,0:T(8,128)} %v_in.1, s32[1,4,4096]{2,1,0:T(4,128)} %rows_in.1, s32[1,4,4096]{2,1,0:T(4,128)} %cols_in.1, f32[1,4,4096]{2,1,0:T(4,128)} %vals_in.1, s32[1,4]{1,0:T(1,128)} %count_in.1), custom_call_target="tpu_custom_call" | custom-call | tf_op jit(solution)/shard_map/pallas_call | solution.py:293
  94.2 0.0 copy-start
  94.2 1.6 %copy.10 = f32[64,512]{1,0:T(8,128)} copy(f32[64,512]{1,0:T(8,128)} %get-tuple-element.4) | data formatting | bytes 262144
  95.8 0.0 copy-done
  95.8 0.7 copy.11
Async XLA Ops:
  94.2 1.6 %copy-start = (f32[64,1024]{1,0:T(8,128)S(1)}, f32[64,1024]{1,0:T(8,128)}, u32[]{:S(2)}) copy-start(f32[64,1024]{1,0:T(8,128)} %get-tuple-element.5) | copy-start | bytes 786436
where the time goes:
time: 96.7 us; the launch traced here: 96.5 us
  Pallas kernels  93.5 us (97%)
  local copies, waits for them, and re-layouts  2.32 us (2%)
    pallas_call x1, Pallas kernels, per_device(): pl.pallas_call(functools.partial(kernel, blocks, ranks), out_shape=(jax.S...  93.5 us
    unnamed x4, local copies, waits for them, and re-layouts  2.32 us

commit v1 on v0

v1 whole, which is shorter than its diff:
```python
import functools

import jax
import jax.numpy as jnp
from jax import lax
from jax.experimental import pallas as pl
from jax.experimental.pallas import tpu as pltpu
from jax.sharding import PartitionSpec as P

BATCH = 1024
LANES = 128
GROUPS = BATCH // LANES
CHUNK = 256
PACK = 16
LEARN_RATE = 0.05
DECAY_WEIGHT = 0.02
MESH = pl.DeviceIdType.MESH


def split_rows(block):
    high = block.astype(jnp.bfloat16)
    low = (block - high.astype(jnp.float32)).astype(jnp.bfloat16)
    return high, low


def kernel(
    blocks, ranks,
    u_in, v_in, rows_in, cols_in, vals_in, count_in,
    u_out, v_out,
    rows, cols, vals, count, users, u_cat, v_cat, held, tiles, chooser, spreader, u_pick, v_pick, u_step, v_step,
    partial, arrived, errs,
    part_send, part_recv, tile_send, tile_recv, user_send, user_recv, load_sem,
):
    depth, user_count = u_in.shape
    item_count = v_in.shape[1]
    strata, tile = rows_in.shape[1:]
    per_tile = tile // BATCH
    spans = tile // LANES
    blk = lax.axis_index("blk")
    rank = lax.axis_index("rank")

    def at_blk(shift):
        return (lax.rem(blk + (shift % blocks), blocks), rank)

    def at_rank(shift):
        return (blk, lax.rem(rank + (shift % ranks), ranks))

    barrier = pltpu.get_barrier_semaphore()
    met = [at_rank(o) for o in range(1, ranks)]
    met += [at_blk(o) for o in range(1, strata)] + [at_blk(-o) for o in range(1, strata)]
    for device in met:
        pl.semaphore_signal(barrier, inc=1, device_id=device, device_id_type=MESH)

    loads = [
        pltpu.make_async_copy(source, target, load_sem.at[i])
        for i, (source, target) in enumerate(
            (
                (count_in, count), (rows_in, rows), (cols_in, cols), (vals_in, vals),
                (u_in, users.at[0]), (v_in, v_out),
            )
        )
    ]
    for load in loads:
        load.start()
    for load in loads[:3]:
        load.wait()

    stratum_at = lax.broadcasted_iota(jnp.int32, (strata, LANES), 0)
    lane_at = lax.broadcasted_iota(jnp.int32, (strata, LANES), 1)
    live = jnp.zeros((strata, LANES), jnp.int32)
    for s in range(strata):
        live = jnp.where(stratum_at == s, count[0, s], live)

    def hold_places(first, last):
        for r in range(first, last):
            here = slice(r * LANES, (r + 1) * LANES)
            alive = lane_at + r * LANES < live
            held[:, r, :] = jnp.where(alive, rows[0, :, here], -1).astype(jnp.float32)
            held[:, spans + r, :] = jnp.where(alive, cols[0, :, here], -1).astype(jnp.float32)

    hold_places(0, GROUPS)
    for first in (0, spans):
        tiles[0, first : first + GROUPS] = held[0, first : first + GROUPS]

    parts = ((0, user_count, 0), (user_count, item_count, spans))
    down = lax.broadcasted_iota(jnp.int16, (PACK, LANES), 0)
    across = lax.broadcasted_iota(jnp.int32, (LANES, LANES), 1)
    ones = jnp.ones((PACK, LANES), jnp.bfloat16)
    zeros = jnp.zeros((PACK, LANES), jnp.bfloat16)

    def index_of(s, q, first):
        at = pl.multiple_of(first + q * GROUPS, GROUPS)
        return tiles[s, pl.ds(at, GROUPS), :].astype(jnp.int32)

    def build_chooser(s, q):
        for base, size, first in parts:
            index = index_of(s, q, first)
            for j in range(GROUPS):
                row = jnp.broadcast_to(index[j : j + 1, :], (PACK, LANES)).astype(jnp.int16)
                for t in range(base, base + size, PACK):
                    chooser[t : t + PACK, j * LANES : (j + 1) * LANES] = jnp.where(down == row, ones, zeros)
                    row = row - jnp.int16(PACK)

    def build_spreader(s, q):
        for base, size, first in parts:
            index = jnp.transpose(index_of(s, q, first))
            for j in range(GROUPS):
                column = jnp.broadcast_to(index[:, j : j + 1], (LANES, LANES))
                for t in range(0, size, LANES):
                    spreader[j * LANES : (j + 1) * LANES, base + t : base + t + LANES] = (
                        jnp.where(across + t == column, 1.0, 0.0).astype(jnp.bfloat16)
                    )

    def store_cat(cat, here, block):
        high, low = split_rows(block)
        cat[:depth, here] = high
        cat[depth:, here] = low

    def cut_users(s):
        store_cat(u_cat, slice(None), users[s])

    def tile_copy(s):
        return pltpu.make_async_remote_copy(
            src_ref=held.at[s], dst_ref=tiles.at[s],
            send_sem=tile_send.at[s], recv_sem=tile_recv.at[s],
            device_id=(lax.rem(blk + blocks - s, blocks), rank),
            device_id_type=MESH,
        )

    def user_copy(s):
        return pltpu.make_async_remote_copy(
            src_ref=users.at[s], dst_ref=users.at[s + 1],
            send_sem=user_send.at[s], recv_sem=user_recv.at[s],
            device_id=at_blk(-1), device_id_type=MESH,
        )

    def home():
        return pltpu.make_async_remote_copy(
            src_ref=users.at[strata - 1], dst_ref=u_out,
            send_sem=user_send.at[strata - 1], recv_sem=user_recv.at[strata - 1],
            device_id=at_blk(strata - 1), device_id_type=MESH,
        )

    def part_copy(slot, o):
        return pltpu.make_async_remote_copy(
            src_ref=partial.at[slot], dst_ref=arrived.at[slot, o - 1],
            send_sem=part_send.at[slot, o - 1], recv_sem=part_recv.at[slot, o - 1],
            device_id=at_rank(o), device_id_type=MESH,
        )

    group_at = lax.broadcasted_iota(jnp.int32, (GROUPS, LANES), 0)

    def pick(cat, rows, c):
        both = jnp.dot(cat[...], chooser[rows, c : c + CHUNK], preferred_element_type=jnp.float32)
        return both[:depth] + both[depth:]

    def pick_items():
        for c in range(0, BATCH, CHUNK):
            v_pick[:, c : c + CHUNK] = pick(v_cat, slice(user_count, None), c)

    def pick_users(slot):
        total = jnp.zeros((GROUPS, LANES), jnp.float32)
        for c in range(0, BATCH, CHUNK):
            here = slice(c, c + CHUNK)
            u = pick(u_cat, slice(0, user_count), c)
            u_pick[:, here] = u
            sums = jnp.sum(u * v_pick[:, here], axis=0, keepdims=True)
            for g in range(0, CHUNK, LANES):
                total = jnp.where(group_at == (c + g) // LANES, sums[:, g : g + LANES], total)
        partial[slot] = total

    def send_parts(slot):
        for o in range(1, ranks):
            part_copy(slot, o).start()

    def get_errors(s, q, slot):
        for o in range(1, ranks):
            part_copy(slot, o).wait_recv()
        total = partial[slot]
        for o in range(1, ranks):
            total = total + arrived[slot, o - 1]
        at = pl.multiple_of(2 * spans + q * GROUPS, GROUPS)
        errs[...] = LEARN_RATE * (tiles[s, pl.ds(at, GROUPS), :] - total)

    def make_steps(mine, other, steps):
        for j in range(GROUPS):
            here = slice(j * LANES, (j + 1) * LANES)
            e = errs[j : j + 1, :]
            high, low = split_rows(e * other[:, here] - LEARN_RATE * DECAY_WEIGHT * mine[:, here])
            steps[:depth, here] = high
            steps[depth:, here] = low

    def spread(steps, first):
        moved = jnp.dot(
            steps[...], spreader[:, first : first + CHUNK], preferred_element_type=jnp.float32
        )
        return moved[:depth] + moved[depth:]

    def move_users(s):
        make_steps(u_pick, v_pick, u_step)
        for t in range(0, user_count, CHUNK):
            here = slice(t, t + CHUNK)
            new = users[s, :, here] + spread(u_step, t)
            users[s, :, here] = new
            store_cat(u_cat, here, new)

    def move_items():
        make_steps(v_pick, u_pick, v_step)
        for t in range(0, item_count, CHUNK):
            here = slice(t, t + CHUNK)
            new = v_out[:, here] + spread(v_step, user_count + t)
            v_out[:, here] = new
            store_cat(v_cat, here, new)

    build_chooser(0, 0)
    for load in loads[4:]:
        load.wait()
    cut_users(0)
    store_cat(v_cat, slice(None), v_out[...])
    pick_items()
    pick_users(0)
    pl.semaphore_wait(barrier, len(met))
    send_parts(0)
    hold_places(GROUPS, spans)
    loads[3].wait()
    for r in range(spans):
        held[:, 2 * spans + r, :] = vals[0, :, r * LANES : (r + 1) * LANES]
    tiles[0] = held[0]
    for s in range(1, strata):
        tile_copy(s).start()

    @pl.loop(0, strata)
    def _(s):
        @pl.loop(0, per_tile - 1)
        def _(q):
            slot = (s * per_tile + q) % 2
            build_spreader(s, q)
            build_chooser(s, q + 1)
            get_errors(s, q, slot)
            move_users(s)
            move_items()
            pick_items()
            pick_users(1 - slot)
            send_parts(1 - slot)
            for o in range(1, ranks):
                part_copy(slot, o).wait_send()

        q = per_tile - 1
        slot = (s * per_tile + q) % 2
        build_spreader(s, q)

        @pl.when(s < strata - 1)
        def _():
            tile_copy(s + 1).wait_recv()
            build_chooser(s + 1, 0)

        get_errors(s, q, slot)
        move_users(s)

        @pl.when(s < strata - 1)
        def _():
            user_copy(s).start()

        @pl.when(s == strata - 1)
        def _():
            home().start()

        move_items()
        for o in range(1, ranks):
            part_copy(slot, o).wait_send()

        @pl.when(s < strata - 1)
        def _():
            pick_items()
            user_copy(s).wait()
            cut_users(s + 1)
            pick_users(1 - slot)
            send_parts(1 - slot)

    for s in range(1, strata):
        tile_copy(s).wait_send()
    home().wait()


def solution(mesh):
    blocks, ranks = mesh.shape["blk"], mesh.shape["rank"]

    def per_device(user_factors, item_factors, tile_rows, tile_cols, tile_vals, tile_count):
        depth, user_count = user_factors.shape
        item_count = item_factors.shape[1]
        strata, tile = tile_rows.shape[1:]
        held = (strata, 3 * tile // LANES, LANES)
        vmem = pl.BlockSpec(memory_space=pltpu.VMEM)
        f32, bf16 = jnp.float32, jnp.bfloat16
        return pl.pallas_call(
            functools.partial(kernel, blocks, ranks),
            out_shape=(
                jax.ShapeDtypeStruct((depth, user_count), f32),
                jax.ShapeDtypeStruct((depth, item_count), f32),
            ),
            in_specs=[pl.BlockSpec(memory_space=pl.ANY)] * 6,
            out_specs=(vmem, vmem),
            scratch_shapes=[
                pltpu.VMEM(tile_rows.shape, jnp.int32),
                pltpu.VMEM(tile_cols.shape, jnp.int32),
                pltpu.VMEM(tile_vals.shape, f32),
                pltpu.SMEM(tile_count.shape, jnp.int32),
                pltpu.VMEM((strata, depth, user_count), f32),
                pltpu.VMEM((2 * depth, user_count), bf16),
                pltpu.VMEM((2 * depth, item_count), bf16),
                pltpu.VMEM(held, f32),
                pltpu.VMEM(held, f32),
                pltpu.VMEM((user_count + item_count, BATCH), bf16),
                pltpu.VMEM((BATCH, user_count + item_count), bf16),
                pltpu.VMEM((depth, BATCH), f32),
                pltpu.VMEM((depth, BATCH), f32),
                pltpu.VMEM((2 * depth, BATCH), bf16),
                pltpu.VMEM((2 * depth, BATCH), bf16),
                pltpu.VMEM((2, GROUPS, LANES), f32),
                pltpu.VMEM((2, ranks - 1, GROUPS, LANES), f32),
                pltpu.VMEM((GROUPS, LANES), f32),
                pltpu.SemaphoreType.DMA((2, ranks - 1)),
                pltpu.SemaphoreType.DMA((2, ranks - 1)),
                pltpu.SemaphoreType.DMA((strata,)),
                pltpu.SemaphoreType.DMA((strata,)),
                pltpu.SemaphoreType.DMA((strata,)),
                pltpu.SemaphoreType.DMA((strata,)),
                pltpu.SemaphoreType.DMA((6,)),
            ],
            compiler_params=pltpu.CompilerParams(
                collective_id=0, has_side_effects=True, vmem_limit_bytes=60 * 1024 * 1024
            ),
        )(user_factors, item_factors, tile_rows, tile_cols, tile_vals, tile_count)

    placed = (
        P("rank", "blk"),
        P("rank", "blk"),
        P("blk", None, None),
        P("blk", None, None),
        P("blk", None, None),
        P("blk", None),
    )
    return jax.shard_map(
        per_device,
        mesh=mesh,
        in_specs=placed,
        out_specs=(P("rank", "blk"), P("rank", "blk")),
        check_vma=False,
    )
```

time: 96.7 us -> 92.4 us (0.956)
  Pallas kernels: 93.5 us -> 89.3 us
    pallas_call x1, Pallas kernels: 93.5 us -> 89.3 us  [per_device(): pl.pallas_call(functools.partial(kernel, blocks, ranks), out_shape=(jax.S...]
where the time goes in v1:
time: 92.4 us; the launch traced here: 92.2 us
  Pallas kernels  89.3 us (97%)
  local copies, waits for them, and re-layouts  2.32 us (3%)
    pallas_call x1, Pallas kernels, per_device(): pl.pallas_call(functools.partial(kernel, blocks, ranks), out_shape=(jax.S...  89.3 us
    unnamed x4, local copies, waits for them, and re-layouts  2.32 us

profile of v1, /device:TPU:0, one launch (start us, length us, event | category | flops | bytes accessed | tf_op | source)
XLA Modules:
  0.0 92.2 jit_solution(7577891657046999320)
XLA Ops:
  0.6 89.3 %shard_map.77 = (f32[64,512]{1,0:T(8,128)}, f32[64,1024]{1,0:T(8,128)}) custom-call(f32[64,512]{1,0:T(8,128)} %u_in.1, f32[64,1024]{1,0:T(8,128)} %v_in.1, s32[1,4,4096]{2,1,0:T(4,128)} %rows_in.1, s32[1,4,4096]{2,1,0:T(4,128)} %cols_in.1, f32[1,4,4096]{2,1,0:T(4,128)} %vals_in.1, s32[1,4]{1,0:T(1,128)} %count_in.1), custom_call_target="tpu_custom_call" | custom-call | tf_op jit(solution)/shard_map/pallas_call | solution.py:295
  89.9 0.0 copy-start
  89.9 1.6 %copy.10 = f32[64,512]{1,0:T(8,128)} copy(f32[64,512]{1,0:T(8,128)} %get-tuple-element.4) | data formatting | bytes 262144
  91.5 0.0 copy-done
  91.5 0.7 copy.11
Async XLA Ops:
  89.9 1.6 %copy-start = (f32[64,1024]{1,0:T(8,128)S(1)}, f32[64,1024]{1,0:T(8,128)}, u32[]{:S(2)}) copy-start(f32[64,1024]{1,0:T(8,128)} %get-tuple-element.5) | copy-start | bytes 786436

commit v2 on v1

--- a/solution.py
+++ b/solution.py
@@ -154,17 +154,27 @@
         both = jnp.dot(cat[...], chooser[rows, c : c + CHUNK], preferred_element_type=jnp.float32)
         return both[:depth] + both[depth:]
 
-    def pick_items():
-        for c in range(0, BATCH, CHUNK):
-            v_pick[:, c : c + CHUNK] = pick(v_cat, slice(user_count, None), c)
-
-    def pick_users(slot):
+    def pick_users(c):
+        here = slice(c, c + CHUNK)
+        u = pick(u_cat, slice(0, user_count), c)
+        u_pick[:, here] = u
+        return u
+
+    def pick_items(c):
+        here = slice(c, c + CHUNK)
+        v = pick(v_cat, slice(user_count, None), c)
+        v_pick[:, here] = v
+        return v
+
+    def predict(slot, users_first):
+        first, second = (pick_users, pick_items) if users_first else (pick_items, pick_users)
+        other = u_pick if users_first else v_pick
+        if users_first:
+            for c in range(0, BATCH, CHUNK):
+                first(c)
         total = jnp.zeros((GROUPS, LANES), jnp.float32)
         for c in range(0, BATCH, CHUNK):
-            here = slice(c, c + CHUNK)
-            u = pick(u_cat, slice(0, user_count), c)
-            u_pick[:, here] = u
-            sums = jnp.sum(u * v_pick[:, here], axis=0, keepdims=True)
+            sums = jnp.sum(second(c) * other[:, c : c + CHUNK], axis=0, keepdims=True)
             for g in range(0, CHUNK, LANES):
                 total = jnp.where(group_at == (c + g) // LANES, sums[:, g : g + LANES], total)
         partial[slot] = total
@@ -217,8 +227,7 @@
         load.wait()
     cut_users(0)
     store_cat(v_cat, slice(None), v_out[...])
-    pick_items()
-    pick_users(0)
+    predict(0, True)
     pl.semaphore_wait(barrier, len(met))
     send_parts(0)
     hold_places(GROUPS, spans)
@@ -239,8 +248,7 @@
             get_errors(s, q, slot)
             move_users(s)
             move_items()
-            pick_items()
-            pick_users(1 - slot)
+            predict(1 - slot, True)
             send_parts(1 - slot)
             for o in range(1, ranks):
                 part_copy(slot, o).wait_send()
@@ -271,15 +279,27 @@
 
         @pl.when(s < strata - 1)
         def _():
-            pick_items()
+            for c in range(0, BATCH, CHUNK):
+                pick_items(c)
             user_copy(s).wait()
             cut_users(s + 1)
-            pick_users(1 - slot)
+            predict(1 - slot, False)
             send_parts(1 - slot)
 
     for s in range(1, strata):
         tile_copy(s).wait_send()
     home().wait()
+
+
+def hand_over(u_in, v_in, u_out, v_out, sem):
+    copies = [
+        pltpu.make_async_copy(source, target, sem.at[i])
+        for i, (source, target) in enumerate(((v_in, v_out), (u_in, u_out)))
+    ]
+    for copy in copies:
+        copy.start()
+    for copy in copies:
+        copy.wait()
 
 
 def solution(mesh):
@@ -292,11 +312,11 @@
         held = (strata, 3 * tile // LANES, LANES)
         vmem = pl.BlockSpec(memory_space=pltpu.VMEM)
         f32, bf16 = jnp.float32, jnp.bfloat16
-        return pl.pallas_call(
+        moved = pl.pallas_call(
             functools.partial(kernel, blocks, ranks),
             out_shape=(
-                jax.ShapeDtypeStruct((depth, user_count), f32),
-                jax.ShapeDtypeStruct((depth, item_count), f32),
+                pltpu.VMEM((depth, user_count), f32),
+                pltpu.VMEM((depth, item_count), f32),
             ),
             in_specs=[pl.BlockSpec(memory_space=pl.ANY)] * 6,
             out_specs=(vmem, vmem),
@@ -331,6 +351,16 @@
                 collective_id=0, has_side_effects=True, vmem_limit_bytes=60 * 1024 * 1024
             ),
         )(user_factors, item_factors, tile_rows, tile_cols, tile_vals, tile_count)
+        return pl.pallas_call(
+            hand_over,
+            out_shape=(
+                jax.ShapeDtypeStruct((depth, user_count), f32),
+                jax.ShapeDtypeStruct((depth, item_count), f32),
+            ),
+            in_specs=[vmem, vmem],
+            out_specs=[pl.BlockSpec(memory_space=pl.ANY)] * 2,
+            scratch_shapes=[pltpu.SemaphoreType.DMA((2,))],
+        )(*[pltpu.with_memory_space_constraint(x, pltpu.VMEM) for x in moved])
 
     placed = (
         P("rank", "blk"),

time: 92.4 us -> 89.3 us (0.966)
  local copies, waits for them, and re-layouts: 2.32 us -> 0 us
    unnamed x4 -> x0, local copies, waits for them, and re-layouts: 2.32 us -> none
    pallas_call x1 -> x2, Pallas kernels: 89.3 us -> 88.5 us  [the longest x1 87.8 us: per_device(): pl.pallas_call(functools.partial(kernel, blocks, ranks), out_shape=(pltpu...]
where the time goes in v2:
time: 89.3 us; the launch traced here: 89.2 us
  Pallas kernels  88.5 us (99%)
    pallas_call x1, Pallas kernels, per_device(): pl.pallas_call(functools.partial(kernel, blocks, ranks), out_shape=(pltpu...  87.8 us

profile of v2, /device:TPU:0, one launch (start us, length us, event | category | flops | bytes accessed | tf_op | source)
XLA Modules:
  0.0 89.2 jit_solution(3907350801459618275)
XLA Ops:
  0.6 87.8 %shard_map.77 = (f32[64,512]{1,0:T(8,128)S(1)}, f32[64,1024]{1,0:T(8,128)S(1)}) custom-call(f32[64,512]{1,0:T(8,128)} %u_in.1, f32[64,1024]{1,0:T(8,128)} %v_in.1, s32[1,4,4096]{2,1,0:T(4,128)} %rows_in.1, s32[1,4,4096]{2,1,0:T(4,128)} %cols_in.1, f32[1,4,4096]{2,1,0:T(4,128)} %vals_in.1, s32[1,4]{1,0:T(1,128)} %count_in.1), custom_call_target="tpu_custom_call" | custom-call | tf_op jit(solution)/shard_map/pallas_call | solution.py:315
  88.4 0.8 shard_map.78

commit v3 on v2

--- a/solution.py
+++ b/solution.py
@@ -12,6 +12,7 @@
 GROUPS = BATCH // LANES
 CHUNK = 256
 PACK = 16
+FOLD = 2
 LEARN_RATE = 0.05
 DECAY_WEIGHT = 0.02
 MESH = pl.DeviceIdType.MESH
@@ -27,7 +28,8 @@
     blocks, ranks,
     u_in, v_in, rows_in, cols_in, vals_in, count_in,
     u_out, v_out,
-    rows, cols, vals, count, users, u_cat, v_cat, held, tiles, chooser, spreader, u_pick, v_pick, u_step, v_step,
+    rows, cols, vals, count, users, u_cat, v_cat, held, tiles, chooser, sides, spreader, u_pick, v_pick, u_next, v_next,
+    u_step, v_step, u_turn, v_turn,
     partial, arrived, errs,
     part_send, part_recv, tile_send, tile_recv, user_send, user_recv, load_sem,
 ):
@@ -36,6 +38,8 @@
     strata, tile = rows_in.shape[1:]
     per_tile = tile // BATCH
     spans = tile // LANES
+    user_keys = user_count // FOLD
+    item_keys = item_count // FOLD
     blk = lax.axis_index("blk")
     rank = lax.axis_index("rank")
 
@@ -44,12 +48,6 @@
 
     def at_rank(shift):
         return (blk, lax.rem(rank + (shift % ranks), ranks))
-
-    barrier = pltpu.get_barrier_semaphore()
-    met = [at_rank(o) for o in range(1, ranks)]
-    met += [at_blk(o) for o in range(1, strata)] + [at_blk(-o) for o in range(1, strata)]
-    for device in met:
-        pl.semaphore_signal(barrier, inc=1, device_id=device, device_id_type=MESH)
 
     loads = [
         pltpu.make_async_copy(source, target, load_sem.at[i])
@@ -62,8 +60,13 @@
     ]
     for load in loads:
         load.start()
-    for load in loads[:3]:
-        load.wait()
+    barrier = pltpu.get_barrier_semaphore()
+    met = [at_rank(o) for o in range(1, ranks)]
+    met += [at_blk(o) for o in range(1, strata)] + [at_blk(-o) for o in range(1, strata)]
+    for device in met:
+        pl.semaphore_signal(barrier, inc=1, device_id=device, device_id_type=MESH)
+    for i in (0, 1, 2, 4, 5):
+        loads[i].wait()
 
     stratum_at = lax.broadcasted_iota(jnp.int32, (strata, LANES), 0)
     lane_at = lax.broadcasted_iota(jnp.int32, (strata, LANES), 1)
@@ -92,9 +95,14 @@
         at = pl.multiple_of(first + q * GROUPS, GROUPS)
         return tiles[s, pl.ds(at, GROUPS), :].astype(jnp.int32)
 
-    def build_chooser(s, q):
-        for base, size, first in parts:
+    folded = ((0, user_keys, 0, 0), (1, item_keys, spans, user_keys))
+
+    def build_chooser(s, q, wanted=folded):
+        for p, size, first, base in wanted:
             index = index_of(s, q, first)
+            side = index >= size
+            sides[p] = jnp.where(side, 1.0, 0.0)
+            index = jnp.where(side, index - size, index)
             for j in range(GROUPS):
                 row = jnp.broadcast_to(index[j : j + 1, :], (PACK, LANES)).astype(jnp.int16)
                 for t in range(base, base + size, PACK):
@@ -111,13 +119,19 @@
                         jnp.where(across + t == column, 1.0, 0.0).astype(jnp.bfloat16)
                     )
 
-    def store_cat(cat, here, block):
-        high, low = split_rows(block)
-        cat[:depth, here] = high
-        cat[depth:, here] = low
-
-    def cut_users(s):
-        store_cat(u_cat, slice(None), users[s])
+    def fold(cat, t, pieces):
+        keys = cat.shape[1]
+        b, at = t // keys, t % keys
+        for i, piece in enumerate(pieces):
+            row = (b * len(pieces) + i) * depth
+            cat[row : row + depth, at : at + CHUNK] = piece
+
+    def cut_users(s, t):
+        fold(u_cat, t, split_rows(users[s, :, t : t + CHUNK]))
+
+    def cut_items():
+        for t in range(0, item_count, CHUNK):
+            fold(v_cat, t, split_rows(v_out[:, t : t + CHUNK]))
 
     def tile_copy(s):
         return pltpu.make_async_remote_copy(
@@ -127,17 +141,19 @@
             device_id_type=MESH,
         )
 
-    def user_copy(s):
+    def user_copy(s, t):
+        here = slice(t, t + CHUNK)
         return pltpu.make_async_remote_copy(
-            src_ref=users.at[s], dst_ref=users.at[s + 1],
-            send_sem=user_send.at[s], recv_sem=user_recv.at[s],
+            src_ref=users.at[s, :, here], dst_ref=users.at[s + 1, :, here],
+            send_sem=user_send.at[s, t // CHUNK], recv_sem=user_recv.at[s, t // CHUNK],
             device_id=at_blk(-1), device_id_type=MESH,
         )
 
-    def home():
+    def home(t):
+        here = slice(t, t + CHUNK)
         return pltpu.make_async_remote_copy(
-            src_ref=users.at[strata - 1], dst_ref=u_out,
-            send_sem=user_send.at[strata - 1], recv_sem=user_recv.at[strata - 1],
+            src_ref=users.at[strata - 1, :, here], dst_ref=u_out.at[:, here],
+            send_sem=user_send.at[strata - 1, t // CHUNK], recv_sem=user_recv.at[strata - 1, t // CHUNK],
             device_id=at_blk(strata - 1), device_id_type=MESH,
         )
 
@@ -150,37 +166,46 @@
 
     group_at = lax.broadcasted_iota(jnp.int32, (GROUPS, LANES), 0)
 
-    def pick(cat, rows, c):
+    user_rows, item_rows = slice(0, user_keys), slice(user_keys, user_keys + item_keys)
+
+    def pick(cat, p, c):
+        rows = (user_rows, item_rows)[p]
         both = jnp.dot(cat[...], chooser[rows, c : c + CHUNK], preferred_element_type=jnp.float32)
-        return both[:depth] + both[depth:]
-
-    def pick_users(c):
-        here = slice(c, c + CHUNK)
-        u = pick(u_cat, slice(0, user_count), c)
-        u_pick[:, here] = u
-        return u
-
-    def pick_items(c):
-        here = slice(c, c + CHUNK)
-        v = pick(v_cat, slice(user_count, None), c)
-        v_pick[:, here] = v
-        return v
-
-    def predict(slot, users_first):
-        first, second = (pick_users, pick_items) if users_first else (pick_items, pick_users)
-        other = u_pick if users_first else v_pick
-        if users_first:
-            for c in range(0, BATCH, CHUNK):
-                first(c)
+        found = []
+        for g in range(0, CHUNK, LANES):
+            j = (c + g) // LANES
+            at = both[:, g : g + LANES]
+            half = at.shape[0] // 2
+            first, second = at[:half], at[half:]
+            if half > depth:
+                first, second = first[:depth] + first[depth:], second[:depth] + second[depth:]
+            side = jnp.broadcast_to(sides[p, j : j + 1, :], (depth, LANES)) > 0.5
+            found.append(jnp.where(side, second, first))
+        return found
+
+    def pick_whole(cat, p, target, c):
+        for g, found in enumerate(pick(cat, p, c)):
+            target[:, c + g * LANES : c + (g + 1) * LANES] = found
+
+    def pick_moved(turned, p, stale, target, c):
+        for g, found in enumerate(pick(turned, p, c)):
+            here = slice(c + g * LANES, c + (g + 1) * LANES)
+            target[:, here] = stale[:, here] + found
+
+    def sum_parts(slot, pick_last):
         total = jnp.zeros((GROUPS, LANES), jnp.float32)
         for c in range(0, BATCH, CHUNK):
-            sums = jnp.sum(second(c) * other[:, c : c + CHUNK], axis=0, keepdims=True)
-            for g in range(0, CHUNK, LANES):
-                total = jnp.where(group_at == (c + g) // LANES, sums[:, g : g + LANES], total)
+            pick_last(c)
+            for j in range(c // LANES, (c + CHUNK) // LANES):
+                here = slice(j * LANES, (j + 1) * LANES)
+                sums = jnp.sum(u_pick[:, here] * v_pick[:, here], axis=0, keepdims=True)
+                total = jnp.where(group_at == j, sums, total)
         partial[slot] = total
 
+    chunks = range(0, BATCH, CHUNK)
+
     def send_parts(slot):
-        for o in range(1, ranks):
+        for o in sorted(range(1, ranks), key=lambda o: abs(o - ranks // 2)):
             part_copy(slot, o).start()
 
     def get_errors(s, q, slot):
@@ -206,28 +231,26 @@
         )
         return moved[:depth] + moved[depth:]
 
-    def move_users(s):
-        make_steps(u_pick, v_pick, u_step)
-        for t in range(0, user_count, CHUNK):
-            here = slice(t, t + CHUNK)
-            new = users[s, :, here] + spread(u_step, t)
-            users[s, :, here] = new
-            store_cat(u_cat, here, new)
-
-    def move_items():
-        make_steps(v_pick, u_pick, v_step)
-        for t in range(0, item_count, CHUNK):
-            here = slice(t, t + CHUNK)
-            new = v_out[:, here] + spread(v_step, user_count + t)
-            v_out[:, here] = new
-            store_cat(v_cat, here, new)
-
-    build_chooser(0, 0)
-    for load in loads[4:]:
-        load.wait()
-    cut_users(0)
-    store_cat(v_cat, slice(None), v_out[...])
-    predict(0, True)
+    def move_users(s, t):
+        here = slice(t, t + CHUNK)
+        moved = spread(u_step, t)
+        users[s, :, here] += moved
+        return moved
+
+    def move_items(t):
+        here = slice(t, t + CHUNK)
+        moved = spread(v_step, user_count + t)
+        v_out[:, here] += moved
+        return moved
+
+    for t in range(0, user_count, CHUNK):
+        cut_users(0, t)
+    build_chooser(0, 0, folded[:1])
+    for c in chunks:
+        pick_whole(u_cat, 0, u_pick, c)
+    cut_items()
+    build_chooser(0, 0, folded[1:])
+    sum_parts(0, lambda c: pick_whole(v_cat, 1, v_pick, c))
     pl.semaphore_wait(barrier, len(met))
     send_parts(0)
     hold_places(GROUPS, spans)
@@ -243,12 +266,24 @@
         @pl.loop(0, per_tile - 1)
         def _(q):
             slot = (s * per_tile + q) % 2
+            for t in range(0, user_count, CHUNK):
+                cut_users(s, t)
+            cut_items()
+            build_chooser(s, q + 1)
+            for c in chunks:
+                pick_whole(u_cat, 0, u_next, c)
+                pick_whole(v_cat, 1, v_next, c)
             build_spreader(s, q)
-            build_chooser(s, q + 1)
             get_errors(s, q, slot)
-            move_users(s)
-            move_items()
-            predict(1 - slot, True)
+            make_steps(u_pick, v_pick, u_step)
+            for t in range(0, user_count, CHUNK):
+                fold(u_turn, t, [move_users(s, t).astype(jnp.bfloat16)])
+            make_steps(v_pick, u_pick, v_step)
+            for t in range(0, item_count, CHUNK):
+                fold(v_turn, t, [move_items(t).astype(jnp.bfloat16)])
+            for c in chunks:
+                pick_moved(u_turn, 0, u_next, u_pick, c)
+            sum_parts(1 - slot, lambda c: pick_moved(v_turn, 1, v_next, v_pick, c))
             send_parts(1 - slot)
             for o in range(1, ranks):
                 part_copy(slot, o).wait_send()
@@ -263,32 +298,39 @@
             build_chooser(s + 1, 0)
 
         get_errors(s, q, slot)
-        move_users(s)
+        make_steps(u_pick, v_pick, u_step)
+        for t in range(0, user_count, CHUNK):
+            move_users(s, t)
+
+            @pl.when(s < strata - 1)
+            def _():
+                user_copy(s, t).start()
+
+            @pl.when(s == strata - 1)
+            def _():
+                home(t).start()
+
+        make_steps(v_pick, u_pick, v_step)
+        for t in range(0, item_count, CHUNK):
+            move_items(t)
+        for o in range(1, ranks):
+            part_copy(slot, o).wait_send()
 
         @pl.when(s < strata - 1)
         def _():
-            user_copy(s).start()
-
-        @pl.when(s == strata - 1)
-        def _():
-            home().start()
-
-        move_items()
-        for o in range(1, ranks):
-            part_copy(slot, o).wait_send()
-
-        @pl.when(s < strata - 1)
-        def _():
-            for c in range(0, BATCH, CHUNK):
-                pick_items(c)
-            user_copy(s).wait()
-            cut_users(s + 1)
-            predict(1 - slot, False)
+            cut_items()
+            for c in chunks:
+                pick_whole(v_cat, 1, v_pick, c)
+            for t in range(0, user_count, CHUNK):
+                user_copy(s, t).wait()
+                cut_users(s + 1, t)
+            sum_parts(1 - slot, lambda c: pick_whole(u_cat, 0, u_pick, c))
             send_parts(1 - slot)
 
     for s in range(1, strata):
         tile_copy(s).wait_send()
-    home().wait()
+    for t in range(0, user_count, CHUNK):
+        home(t).wait()
 
 
 def hand_over(u_in, v_in, u_out, v_out, sem):
@@ -326,16 +368,21 @@
                 pltpu.VMEM(tile_vals.shape, f32),
                 pltpu.SMEM(tile_count.shape, jnp.int32),
                 pltpu.VMEM((strata, depth, user_count), f32),
-                pltpu.VMEM((2 * depth, user_count), bf16),
-                pltpu.VMEM((2 * depth, item_count), bf16),
+                pltpu.VMEM((2 * FOLD * depth, user_count // FOLD), bf16),
+                pltpu.VMEM((2 * FOLD * depth, item_count // FOLD), bf16),
                 pltpu.VMEM(held, f32),
                 pltpu.VMEM(held, f32),
-                pltpu.VMEM((user_count + item_count, BATCH), bf16),
+                pltpu.VMEM(((user_count + item_count) // FOLD, BATCH), bf16),
+                pltpu.VMEM((2, GROUPS, LANES), f32),
                 pltpu.VMEM((BATCH, user_count + item_count), bf16),
+                pltpu.VMEM((depth, BATCH), f32),
+                pltpu.VMEM((depth, BATCH), f32),
                 pltpu.VMEM((depth, BATCH), f32),
                 pltpu.VMEM((depth, BATCH), f32),
                 pltpu.VMEM((2 * depth, BATCH), bf16),
                 pltpu.VMEM((2 * depth, BATCH), bf16),
+                pltpu.VMEM((FOLD * depth, user_count // FOLD), bf16),
+                pltpu.VMEM((FOLD * depth, item_count // FOLD), bf16),
                 pltpu.VMEM((2, GROUPS, LANES), f32),
                 pltpu.VMEM((2, ranks - 1, GROUPS, LANES), f32),
                 pltpu.VMEM((GROUPS, LANES), f32),
@@ -343,8 +390,8 @@
                 pltpu.SemaphoreType.DMA((2, ranks - 1)),
                 pltpu.SemaphoreType.DMA((strata,)),
                 pltpu.SemaphoreType.DMA((strata,)),
-                pltpu.SemaphoreType.DMA((strata,)),
-                pltpu.SemaphoreType.DMA((strata,)),
+                pltpu.SemaphoreType.DMA((strata, user_count // CHUNK)),
+                pltpu.SemaphoreType.DMA((strata, user_count // CHUNK)),
                 pltpu.SemaphoreType.DMA((6,)),
             ],
             compiler_params=pltpu.CompilerParams(

time: 89.3 us -> 86.9 us (0.973)
  Pallas kernels: 88.5 us -> 86.1 us
    pallas_call x1, Pallas kernels: 87.8 us -> 85.4 us  [per_device(): pl.pallas_call(functools.partial(kernel, blocks, ranks), out_shape=(pltpu...]
where the time goes in v3:
time: 86.9 us; the launch traced here: 86.8 us
  Pallas kernels  86.1 us (99%)
    pallas_call x1, Pallas kernels, per_device(): pl.pallas_call(functools.partial(kernel, blocks, ranks), out_shape=(pltpu...  85.4 us

profile of v3, /device:TPU:0, one launch (start us, length us, event | category | flops | bytes accessed | tf_op | source)
XLA Modules:
  0.0 86.8 jit_solution(12565395519119776427)
XLA Ops:
  0.6 85.4 %shard_map.77 = (f32[64,512]{1,0:T(8,128)S(1)}, f32[64,1024]{1,0:T(8,128)S(1)}) custom-call(f32[64,512]{1,0:T(8,128)} %u_in.1, f32[64,1024]{1,0:T(8,128)} %v_in.1, s32[1,4,4096]{2,1,0:T(4,128)} %rows_in.1, s32[1,4,4096]{2,1,0:T(4,128)} %cols_in.1, f32[1,4,4096]{2,1,0:T(4,128)} %vals_in.1, s32[1,4]{1,0:T(1,128)} %count_in.1), custom_call_target="tpu_custom_call" | custom-call | tf_op jit(solution)/shard_map/pallas_call | solution.py:357
  86.0 0.8 shard_map.78

commit v4 on v3

--- a/solution.py
+++ b/solution.py
@@ -28,8 +28,8 @@
     blocks, ranks,
     u_in, v_in, rows_in, cols_in, vals_in, count_in,
     u_out, v_out,
-    rows, cols, vals, count, users, u_cat, v_cat, held, tiles, chooser, sides, spreader, u_pick, v_pick, u_next, v_next,
-    u_step, v_step, u_turn, v_turn,
+    rows, cols, vals, count, users, u_cat, v_cat, held, tiles, chooser, sides, spreader, u_pick, v_pick,
+    u_step, v_step, u_turn, v_turn, u_moved, v_moved,
     partial, arrived, errs,
     part_send, part_recv, tile_send, tile_recv, user_send, user_recv, load_sem,
 ):
@@ -97,11 +97,11 @@
 
     folded = ((0, user_keys, 0, 0), (1, item_keys, spans, user_keys))
 
-    def build_chooser(s, q, wanted=folded):
+    def build_chooser(slot, s, q, wanted=folded):
         for p, size, first, base in wanted:
             index = index_of(s, q, first)
             side = index >= size
-            sides[p] = jnp.where(side, 1.0, 0.0)
+            sides[slot, p] = jnp.where(side, 1.0, 0.0)
             index = jnp.where(side, index - size, index)
             for j in range(GROUPS):
                 row = jnp.broadcast_to(index[j : j + 1, :], (PACK, LANES)).astype(jnp.int16)
@@ -110,8 +110,9 @@
                     row = row - jnp.int16(PACK)
 
     def build_spreader(s, q):
-        for base, size, first in parts:
-            index = jnp.transpose(index_of(s, q, first))
+        for p, size, first, base in folded:
+            index = index_of(s, q, first)
+            index = jnp.transpose(jnp.where(index >= size, index - size, index))
             for j in range(GROUPS):
                 column = jnp.broadcast_to(index[:, j : j + 1], (LANES, LANES))
                 for t in range(0, size, LANES):
@@ -168,29 +169,30 @@
 
     user_rows, item_rows = slice(0, user_keys), slice(user_keys, user_keys + item_keys)
 
-    def pick(cat, p, c):
+    def side_of(slot, p, j):
+        return jnp.broadcast_to(sides[slot, p, j : j + 1, :], (depth, LANES))
+
+    def pick(cat, slot, p, c):
         rows = (user_rows, item_rows)[p]
         both = jnp.dot(cat[...], chooser[rows, c : c + CHUNK], preferred_element_type=jnp.float32)
         found = []
         for g in range(0, CHUNK, LANES):
-            j = (c + g) // LANES
             at = both[:, g : g + LANES]
             half = at.shape[0] // 2
             first, second = at[:half], at[half:]
             if half > depth:
                 first, second = first[:depth] + first[depth:], second[:depth] + second[depth:]
-            side = jnp.broadcast_to(sides[p, j : j + 1, :], (depth, LANES)) > 0.5
-            found.append(jnp.where(side, second, first))
+            found.append(jnp.where(side_of(slot, p, (c + g) // LANES) > 0.5, second, first))
         return found
 
-    def pick_whole(cat, p, target, c):
-        for g, found in enumerate(pick(cat, p, c)):
-            target[:, c + g * LANES : c + (g + 1) * LANES] = found
-
-    def pick_moved(turned, p, stale, target, c):
-        for g, found in enumerate(pick(turned, p, c)):
+    def pick_whole(cat, slot, p, target, c):
+        for g, found in enumerate(pick(cat, slot, p, c)):
+            target[slot, :, c + g * LANES : c + (g + 1) * LANES] = found
+
+    def pick_moved(turned, slot, p, target, c):
+        for g, found in enumerate(pick(turned, slot, p, c)):
             here = slice(c + g * LANES, c + (g + 1) * LANES)
-            target[:, here] = stale[:, here] + found
+            target[slot, :, here] += found
 
     def sum_parts(slot, pick_last):
         total = jnp.zeros((GROUPS, LANES), jnp.float32)
@@ -198,7 +200,7 @@
             pick_last(c)
             for j in range(c // LANES, (c + CHUNK) // LANES):
                 here = slice(j * LANES, (j + 1) * LANES)
-                sums = jnp.sum(u_pick[:, here] * v_pick[:, here], axis=0, keepdims=True)
+                sums = jnp.sum(u_pick[slot, :, here] * v_pick[slot, :, here], axis=0, keepdims=True)
                 total = jnp.where(group_at == j, sums, total)
         partial[slot] = total
 
@@ -217,40 +219,51 @@
         at = pl.multiple_of(2 * spans + q * GROUPS, GROUPS)
         errs[...] = LEARN_RATE * (tiles[s, pl.ds(at, GROUPS), :] - total)
 
-    def make_steps(mine, other, steps):
+    def make_steps(slot, p, steps, wanted=(0, 1)):
+        mine, other = ((u_pick, v_pick), (v_pick, u_pick))[p]
         for j in range(GROUPS):
             here = slice(j * LANES, (j + 1) * LANES)
             e = errs[j : j + 1, :]
-            high, low = split_rows(e * other[:, here] - LEARN_RATE * DECAY_WEIGHT * mine[:, here])
-            steps[:depth, here] = high
-            steps[depth:, here] = low
+            pieces = split_rows(e * other[slot, :, here] - LEARN_RATE * DECAY_WEIGHT * mine[slot, :, here])
+            side = side_of(slot, p, j).astype(jnp.bfloat16)
+            for w in wanted:
+                second = pieces[w] * side
+                row = FOLD * depth * w
+                steps[row : row + depth, here] = pieces[w] - second
+                steps[row + depth : row + 2 * depth, here] = second
 
     def spread(steps, first):
-        moved = jnp.dot(
-            steps[...], spreader[:, first : first + CHUNK], preferred_element_type=jnp.float32
-        )
-        return moved[:depth] + moved[depth:]
-
-    def move_users(s, t):
-        here = slice(t, t + CHUNK)
-        moved = spread(u_step, t)
-        users[s, :, here] += moved
-        return moved
-
-    def move_items(t):
-        here = slice(t, t + CHUNK)
-        moved = spread(v_step, user_count + t)
-        v_out[:, here] += moved
-        return moved
+        return jnp.dot(steps, spreader[:, first : first + CHUNK], preferred_element_type=jnp.float32)
+
+    def add_users(s, t, change):
+        for b in range(FOLD):
+            here = slice(b * user_keys + t, b * user_keys + t + CHUNK)
+            users[s, :, here] += change[b * depth : (b + 1) * depth]
+
+    def add_items(t, change):
+        for b in range(FOLD):
+            here = slice(b * item_keys + t, b * item_keys + t + CHUNK)
+            v_out[:, here] += change[b * depth : (b + 1) * depth]
+
+    highs, lows = slice(0, FOLD * depth), slice(FOLD * depth, 2 * FOLD * depth)
+
+    def spread_both(steps, first):
+        change = spread(steps[...], first)
+        return change[highs] + change[lows]
+
+    def turn_part(steps, base, t, moved, turned):
+        change = spread(steps[highs], base + t)
+        moved[:, t : t + CHUNK] = change
+        turned[:, t : t + CHUNK] = change.astype(jnp.bfloat16)
 
     for t in range(0, user_count, CHUNK):
         cut_users(0, t)
-    build_chooser(0, 0, folded[:1])
+    build_chooser(0, 0, 0, folded[:1])
     for c in chunks:
-        pick_whole(u_cat, 0, u_pick, c)
+        pick_whole(u_cat, 0, 0, u_pick, c)
     cut_items()
-    build_chooser(0, 0, folded[1:])
-    sum_parts(0, lambda c: pick_whole(v_cat, 1, v_pick, c))
+    build_chooser(0, 0, 0, folded[1:])
+    sum_parts(0, lambda c: pick_whole(v_cat, 0, 1, v_pick, c))
     pl.semaphore_wait(barrier, len(met))
     send_parts(0)
     hold_places(GROUPS, spans)
@@ -266,25 +279,31 @@
         @pl.loop(0, per_tile - 1)
         def _(q):
             slot = (s * per_tile + q) % 2
+            build_chooser(1 - slot, s, q + 1)
+            for c in chunks:
+                pick_whole(u_cat, 1 - slot, 0, u_pick, c)
+                pick_whole(v_cat, 1 - slot, 1, v_pick, c)
+            build_spreader(s, q)
+            get_errors(s, q, slot)
+            make_steps(slot, 0, u_step, (0,))
+            for t in range(0, user_keys, CHUNK):
+                turn_part(u_step, 0, t, u_moved, u_turn)
+            make_steps(slot, 1, v_step, (0,))
+            for t in range(0, item_keys, CHUNK):
+                turn_part(v_step, user_keys, t, v_moved, v_turn)
+            for c in chunks:
+                pick_moved(u_turn, 1 - slot, 0, u_pick, c)
+            sum_parts(1 - slot, lambda c: pick_moved(v_turn, 1 - slot, 1, v_pick, c))
+            send_parts(1 - slot)
+            make_steps(slot, 0, u_step, (1,))
+            make_steps(slot, 1, v_step, (1,))
+            for t in range(0, user_keys, CHUNK):
+                add_users(s, t, u_moved[:, t : t + CHUNK] + spread(u_step[lows], t))
             for t in range(0, user_count, CHUNK):
                 cut_users(s, t)
+            for t in range(0, item_keys, CHUNK):
+                add_items(t, v_moved[:, t : t + CHUNK] + spread(v_step[lows], user_keys + t))
             cut_items()
-            build_chooser(s, q + 1)
-            for c in chunks:
-                pick_whole(u_cat, 0, u_next, c)
-                pick_whole(v_cat, 1, v_next, c)
-            build_spreader(s, q)
-            get_errors(s, q, slot)
-            make_steps(u_pick, v_pick, u_step)
-            for t in range(0, user_count, CHUNK):
-                fold(u_turn, t, [move_users(s, t).astype(jnp.bfloat16)])
-            make_steps(v_pick, u_pick, v_step)
-            for t in range(0, item_count, CHUNK):
-                fold(v_turn, t, [move_items(t).astype(jnp.bfloat16)])
-            for c in chunks:
-                pick_moved(u_turn, 0, u_next, u_pick, c)
-            sum_parts(1 - slot, lambda c: pick_moved(v_turn, 1, v_next, v_pick, c))
-            send_parts(1 - slot)
             for o in range(1, ranks):
                 part_copy(slot, o).wait_send()
 
@@ -295,24 +314,26 @@
         @pl.when(s < strata - 1)
         def _():
             tile_copy(s + 1).wait_recv()
-            build_chooser(s + 1, 0)
+            build_chooser(1 - slot, s + 1, 0)
 
         get_errors(s, q, slot)
-        make_steps(u_pick, v_pick, u_step)
-        for t in range(0, user_count, CHUNK):
-            move_users(s, t)
-
-            @pl.when(s < strata - 1)
-            def _():
+        make_steps(slot, 0, u_step)
+        for t in range(0, user_keys, CHUNK):
+            add_users(s, t, spread_both(u_step, t))
+
+        @pl.when(s < strata - 1)
+        def _():
+            for t in range(0, user_count, CHUNK):
                 user_copy(s, t).start()
 
-            @pl.when(s == strata - 1)
-            def _():
+        @pl.when(s == strata - 1)
+        def _():
+            for t in range(0, user_count, CHUNK):
                 home(t).start()
 
-        make_steps(v_pick, u_pick, v_step)
-        for t in range(0, item_count, CHUNK):
-            move_items(t)
+        make_steps(slot, 1, v_step)
+        for t in range(0, item_keys, CHUNK):
+            add_items(t, spread_both(v_step, user_keys + t))
         for o in range(1, ranks):
             part_copy(slot, o).wait_send()
 
@@ -320,11 +341,11 @@
         def _():
             cut_items()
             for c in chunks:
-                pick_whole(v_cat, 1, v_pick, c)
+                pick_whole(v_cat, 1 - slot, 1, v_pick, c)
             for t in range(0, user_count, CHUNK):
                 user_copy(s, t).wait()
                 cut_users(s + 1, t)
-            sum_parts(1 - slot, lambda c: pick_whole(u_cat, 0, u_pick, c))
+            sum_parts(1 - slot, lambda c: pick_whole(u_cat, 1 - slot, 0, u_pick, c))
             send_parts(1 - slot)
 
     for s in range(1, strata):
@@ -373,16 +394,16 @@
                 pltpu.VMEM(held, f32),
                 pltpu.VMEM(held, f32),
                 pltpu.VMEM(((user_count + item_count) // FOLD, BATCH), bf16),
-                pltpu.VMEM((2, GROUPS, LANES), f32),
-                pltpu.VMEM((BATCH, user_count + item_count), bf16),
-                pltpu.VMEM((depth, BATCH), f32),
-                pltpu.VMEM((depth, BATCH), f32),
-                pltpu.VMEM((depth, BATCH), f32),
-                pltpu.VMEM((depth, BATCH), f32),
-                pltpu.VMEM((2 * depth, BATCH), bf16),
-                pltpu.VMEM((2 * depth, BATCH), bf16),
+                pltpu.VMEM((2, 2, GROUPS, LANES), f32),
+                pltpu.VMEM((BATCH, (user_count + item_count) // FOLD), bf16),
+                pltpu.VMEM((2, depth, BATCH), f32),
+                pltpu.VMEM((2, depth, BATCH), f32),
+                pltpu.VMEM((2 * FOLD * depth, BATCH), bf16),
+                pltpu.VMEM((2 * FOLD * depth, BATCH), bf16),
                 pltpu.VMEM((FOLD * depth, user_count // FOLD), bf16),
                 pltpu.VMEM((FOLD * depth, item_count // FOLD), bf16),
+                pltpu.VMEM((FOLD * depth, user_count // FOLD), f32),
+                pltpu.VMEM((FOLD * depth, item_count // FOLD), f32),
                 pltpu.VMEM((2, GROUPS, LANES), f32),
                 pltpu.VMEM((2, ranks - 1, GROUPS, LANES), f32),
                 pltpu.VMEM((GROUPS, LANES), f32),

time: 86.9 us -> 85 us (0.978)
  Pallas kernels: 86.1 us -> 84.2 us
    pallas_call x1, Pallas kernels: 85.4 us -> 83.4 us  [per_device(): pl.pallas_call(functools.partial(kernel, blocks, ranks), out_shape=(pltpu...]
where the time goes in v4:
time: 85 us; the launch traced here: 84.8 us
  Pallas kernels  84.2 us (99%)
    pallas_call x1, Pallas kernels, per_device(): pl.pallas_call(functools.partial(kernel, blocks, ranks), out_shape=(pltpu...  83.4 us

profile of v4, /device:TPU:0, one launch (start us, length us, event | category | flops | bytes accessed | tf_op | source)
XLA Modules:
  0.0 84.8 jit_solution(14624552118281679682)
XLA Ops:
  0.6 83.4 %shard_map.77 = (f32[64,512]{1,0:T(8,128)S(1)}, f32[64,1024]{1,0:T(8,128)S(1)}) custom-call(f32[64,512]{1,0:T(8,128)} %u_in.1, f32[64,1024]{1,0:T(8,128)} %v_in.1, s32[1,4,4096]{2,1,0:T(4,128)} %rows_in.1, s32[1,4,4096]{2,1,0:T(4,128)} %cols_in.1, f32[1,4,4096]{2,1,0:T(4,128)} %vals_in.1, s32[1,4]{1,0:T(1,128)} %count_in.1), custom_call_target="tpu_custom_call" | custom-call | tf_op jit(solution)/shard_map/pallas_call | solution.py:378
  84.0 0.8 shard_map.78

commit v5 on v4

--- a/solution.py
+++ b/solution.py
@@ -285,15 +285,15 @@
                 pick_whole(v_cat, 1 - slot, 1, v_pick, c)
             build_spreader(s, q)
             get_errors(s, q, slot)
+            make_steps(slot, 1, v_step, (0,))
+            for t in range(0, item_keys, CHUNK):
+                turn_part(v_step, user_keys, t, v_moved, v_turn)
             make_steps(slot, 0, u_step, (0,))
             for t in range(0, user_keys, CHUNK):
                 turn_part(u_step, 0, t, u_moved, u_turn)
-            make_steps(slot, 1, v_step, (0,))
-            for t in range(0, item_keys, CHUNK):
-                turn_part(v_step, user_keys, t, v_moved, v_turn)
             for c in chunks:
-                pick_moved(u_turn, 1 - slot, 0, u_pick, c)
-            sum_parts(1 - slot, lambda c: pick_moved(v_turn, 1 - slot, 1, v_pick, c))
+                pick_moved(v_turn, 1 - slot, 1, v_pick, c)
+            sum_parts(1 - slot, lambda c: pick_moved(u_turn, 1 - slot, 0, u_pick, c))
             send_parts(1 - slot)
             make_steps(slot, 0, u_step, (1,))
             make_steps(slot, 1, v_step, (1,))

time: 85 us -> 84.7 us (level)
  no operation moved by 1% of the time
where the time goes in v5:
time: 84.7 us; the launch traced here: 84.6 us
  Pallas kernels  83.9 us (99%)
    pallas_call x1, Pallas kernels, per_device(): pl.pallas_call(functools.partial(kernel, blocks, ranks), out_shape=(pltpu...  83.2 us

profile of v5, /device:TPU:0, one launch (start us, length us, event | category | flops | bytes accessed | tf_op | source)
XLA Modules:
  0.0 84.6 jit_solution(15537509648066121195)
XLA Ops:
  0.6 83.2 %shard_map.77 = (f32[64,512]{1,0:T(8,128)S(1)}, f32[64,1024]{1,0:T(8,128)S(1)}) custom-call(f32[64,512]{1,0:T(8,128)} %u_in.1, f32[64,1024]{1,0:T(8,128)} %v_in.1, s32[1,4,4096]{2,1,0:T(4,128)} %rows_in.1, s32[1,4,4096]{2,1,0:T(4,128)} %cols_in.1, f32[1,4,4096]{2,1,0:T(4,128)} %vals_in.1, s32[1,4]{1,0:T(1,128)} %count_in.1), custom_call_target="tpu_custom_call" | custom-call | tf_op jit(solution)/shard_map/pallas_call | solution.py:378
  83.8 0.8 shard_map.78

commit v6 on v5

--- a/solution.py
+++ b/solution.py
@@ -147,15 +147,8 @@
         return pltpu.make_async_remote_copy(
             src_ref=users.at[s, :, here], dst_ref=users.at[s + 1, :, here],
             send_sem=user_send.at[s, t // CHUNK], recv_sem=user_recv.at[s, t // CHUNK],
-            device_id=at_blk(-1), device_id_type=MESH,
-        )
-
-    def home(t):
-        here = slice(t, t + CHUNK)
-        return pltpu.make_async_remote_copy(
-            src_ref=users.at[strata - 1, :, here], dst_ref=u_out.at[:, here],
-            send_sem=user_send.at[strata - 1, t // CHUNK], recv_sem=user_recv.at[strata - 1, t // CHUNK],
-            device_id=at_blk(strata - 1), device_id_type=MESH,
+            device_id=(lax.rem(blk + blocks - 1 + s // (strata - 1) * strata, blocks), rank),
+            device_id_type=MESH,
         )
 
     def part_copy(slot, o):
@@ -184,6 +177,13 @@
                 first, second = first[:depth] + first[depth:], second[:depth] + second[depth:]
             found.append(jnp.where(side_of(slot, p, (c + g) // LANES) > 0.5, second, first))
         return found
+
+    def pick_half(b, c):
+        rows = slice(2 * b * depth, 2 * (b + 1) * depth)
+        both = jnp.dot(
+            u_cat[rows, :], chooser[user_rows, c : c + CHUNK], preferred_element_type=jnp.float32
+        )
+        return both[:depth] + both[depth:]
 
     def pick_whole(cat, slot, p, target, c):
         for g, found in enumerate(pick(cat, slot, p, c)):
@@ -320,17 +320,8 @@
         make_steps(slot, 0, u_step)
         for t in range(0, user_keys, CHUNK):
             add_users(s, t, spread_both(u_step, t))
-
-        @pl.when(s < strata - 1)
-        def _():
-            for t in range(0, user_count, CHUNK):
-                user_copy(s, t).start()
-
-        @pl.when(s == strata - 1)
-        def _():
-            for t in range(0, user_count, CHUNK):
-                home(t).start()
-
+        for t in range(0, user_count, CHUNK):
+            user_copy(s, t).start()
         make_steps(slot, 1, v_step)
         for t in range(0, item_keys, CHUNK):
             add_items(t, spread_both(v_step, user_keys + t))
@@ -342,16 +333,32 @@
             cut_items()
             for c in chunks:
                 pick_whole(v_cat, 1 - slot, 1, v_pick, c)
-            for t in range(0, user_count, CHUNK):
+            user_copy(s, 0).wait()
+            cut_users(s + 1, 0)
+            for c in chunks:
+                here = slice(c, c + CHUNK)
+                u_pick[1 - slot, :, here] = pick_half(0, c)
+            for t in range(CHUNK, user_count, CHUNK):
                 user_copy(s, t).wait()
                 cut_users(s + 1, t)
-            sum_parts(1 - slot, lambda c: pick_whole(u_cat, 1 - slot, 0, u_pick, c))
+
+            def pick_rest(c):
+                second = pick_half(1, c)
+                for g in range(0, CHUNK, LANES):
+                    here = slice(c + g, c + g + LANES)
+                    side = side_of(1 - slot, 0, (c + g) // LANES) > 0.5
+                    u_pick[1 - slot, :, here] = jnp.where(
+                        side, second[:, g : g + LANES], u_pick[1 - slot, :, here]
+                    )
+
+            sum_parts(1 - slot, pick_rest)
             send_parts(1 - slot)
 
     for s in range(1, strata):
         tile_copy(s).wait_send()
     for t in range(0, user_count, CHUNK):
-        home(t).wait()
+        user_copy(strata - 1, t).wait()
+        u_out[:, t : t + CHUNK] = users[strata, :, t : t + CHUNK]
 
 
 def hand_over(u_in, v_in, u_out, v_out, sem):
@@ -388,7 +395,7 @@
                 pltpu.VMEM(tile_cols.shape, jnp.int32),
                 pltpu.VMEM(tile_vals.shape, f32),
                 pltpu.SMEM(tile_count.shape, jnp.int32),
-                pltpu.VMEM((strata, depth, user_count), f32),
+                pltpu.VMEM((strata + 1, depth, user_count), f32),
                 pltpu.VMEM((2 * FOLD * depth, user_count // FOLD), bf16),
                 pltpu.VMEM((2 * FOLD * depth, item_count // FOLD), bf16),
                 pltpu.VMEM(held, f32),

time: 84.7 us -> 84.5 us (level)
  no operation moved by 1% of the time
where the time goes in v6:
time: 84.5 us; the launch traced here: 84.4 us
  Pallas kernels  83.7 us (99%)
    pallas_call x1, Pallas kernels, per_device(): pl.pallas_call(functools.partial(kernel, blocks, ranks), out_shape=(pltpu...  83 us

profile of v6, /device:TPU:0, one launch (start us, length us, event | category | flops | bytes accessed | tf_op | source)
XLA Modules:
  0.0 84.4 jit_solution(15454555756148873178)
XLA Ops:
  0.6 83.0 %shard_map.77 = (f32[64,512]{1,0:T(8,128)S(1)}, f32[64,1024]{1,0:T(8,128)S(1)}) custom-call(f32[64,512]{1,0:T(8,128)} %u_in.1, f32[64,1024]{1,0:T(8,128)} %v_in.1, s32[1,4,4096]{2,1,0:T(4,128)} %rows_in.1, s32[1,4,4096]{2,1,0:T(4,128)} %cols_in.1, f32[1,4,4096]{2,1,0:T(4,128)} %vals_in.1, s32[1,4]{1,0:T(1,128)} %count_in.1), custom_call_target="tpu_custom_call" | custom-call | tf_op jit(solution)/shard_map/pallas_call | solution.py:385
  83.6 0.8 shard_map.78

commit v7 on v6

--- a/solution.py
+++ b/solution.py
@@ -286,9 +286,9 @@
             build_spreader(s, q)
             get_errors(s, q, slot)
             make_steps(slot, 1, v_step, (0,))
+            make_steps(slot, 0, u_step, (0,))
             for t in range(0, item_keys, CHUNK):
                 turn_part(v_step, user_keys, t, v_moved, v_turn)
-            make_steps(slot, 0, u_step, (0,))
             for t in range(0, user_keys, CHUNK):
                 turn_part(u_step, 0, t, u_moved, u_turn)
             for c in chunks:

time: 84.5 us -> 84.5 us (level)
  no operation moved by 1% of the time
where the time goes in v7:
time: 84.5 us; the launch traced here: 84.4 us
  Pallas kernels  83.7 us (99%)
    pallas_call x1, Pallas kernels, per_device(): pl.pallas_call(functools.partial(kernel, blocks, ranks), out_shape=(pltpu...  83 us

profile of v7, /device:TPU:0, one launch (start us, length us, event | category | flops | bytes accessed | tf_op | source)
XLA Modules:
  0.0 84.4 jit_solution(15454555756148873178)
XLA Ops:
  0.6 83.0 %shard_map.77 = (f32[64,512]{1,0:T(8,128)S(1)}, f32[64,1024]{1,0:T(8,128)S(1)}) custom-call(f32[64,512]{1,0:T(8,128)} %u_in.1, f32[64,1024]{1,0:T(8,128)} %v_in.1, s32[1,4,4096]{2,1,0:T(4,128)} %rows_in.1, s32[1,4,4096]{2,1,0:T(4,128)} %cols_in.1, f32[1,4,4096]{2,1,0:T(4,128)} %vals_in.1, s32[1,4]{1,0:T(1,128)} %count_in.1), custom_call_target="tpu_custom_call" | custom-call | tf_op jit(solution)/shard_map/pallas_call | solution.py:385
  83.6 0.8 shard_map.78
